TPU v7x, 32 devices: a whole 2x2x4 slice. The times are simulated.
32 devices in a mesh: groups: 2 (over y), cache: 4 (over z), blk: 4 (over x, core).
Axes of the slice: x: 2, y: 2, z: 4, core: 2. Of those that a mesh axis runs over, the one named last changes fastest.
Arguments:
- queries: bfloat16 [8, 512, 2048], P(('groups', 'cache'), 'blk'), parts along dimension 0, may hold values from -6 to 6
- kv_new: bfloat16 [8, 512, 1024], P(('groups', 'cache'), 'blk'), parts along dimension 0, may hold values from -6 to 6
- page_pool: bfloat16 [8, 128, 8, 1024], P(('groups', 'cache')), parts along dimension 0, may hold values from -6 to 6
- page_owner: int32 [8, 4, 32, 1], P(('groups', 'cache'), 'blk'), parts along dimension 0, may hold values from 0 to 3; in each aligned block of 32 rows (0 to 31, 32 to 63, ..., all dimensions but the last counted through in order) at most 16 rows name the same one
- page_slot: int32 [8, 4, 32], P(('groups', 'cache'), 'blk'), parts along dimension 0, may hold values from 0 to 127
- prefix_len: int32 [8], P(('groups', 'cache')), parts along dimension 0, may hold values from 1 to 1024, 2048 in all
- suffix_len: int32 [8], P(('groups', 'cache')), parts along dimension 0, may hold values from 1 to 512, 1536 in all
- ssm_in: bfloat16 [8, 512, 2048], P(('groups', 'cache'), 'blk'), parts along dimension 0, may hold values from -6 to 6
- b_in: bfloat16 [8, 512, 128], P(('groups', 'cache'), 'blk'), parts along dimension 0, may hold values from -4 to 4
- c_in: bfloat16 [8, 512, 128], P(('groups', 'cache'), 'blk'), parts along dimension 0, may hold values from -4 to 4
- step_size: float32 [8, 512, 32], P(('groups', 'cache'), 'blk'), parts along dimension 0, may hold values from 0.01 to 0.1
- decay_rate: float32 [32], replicated, may hold values from 0.001953125 to 4
- skip_gain: float32 [32], replicated, may hold values from 0.5 to 1.5
- prior_state: float32 [8, 32, 64, 128], P(('groups', 'cache')), parts along dimension 0, may hold values from -4 to 4
Outputs:
- attn_out: bfloat16 [8, 512, 2048], P(('groups', 'cache'), 'blk'), parts along dimension 0
- ssm_out: bfloat16 [8, 512, 2048], P(('groups', 'cache'), 'blk'), parts along dimension 0
There are 2 independent parts, one for each index of `groups`. A program takes and returns all parts, laid end to end along the dimension named above; an argument that names none is the same for every part. Nothing has to cross between parts.
Inputs may be any that keep to these rules, and one draw needn't show every extreme that they name: `page_owner`: among the 32 pages of one request at one index of blk, no owner is named more than 16 times, a bound that some block reaches. `prefix_len`: the largest is 1024. `suffix_len`: the largest is 512.
All inputs are finite; a program needn't handle non-finite values. No bound on the sum of `prefix_len` or of `suffix_len` on one device may be relied on, other than what follows from the above.
Results may differ from a plain program's by a relative error of at most 0.008.
Values may be sent and summed in bfloat16 or wider, within the bound.
A program may use at most 128 MiB of HBM per device.

v0:
```python
import math
import jax
import jax.numpy as jnp
from jax import lax
from jax.sharding import PartitionSpec as P

QH = 16
KVH = 4
HD = 128
SH = 32
HP = 64
NS = 128
PAGE = 8
LIST = 32
NEG = -1e30


def passed_along(value, axis, steps):
    count = lax.axis_size(axis)
    leading, last = (max(0, -steps), min(count, count - steps))
    return lax.ppermute(value, axis, [(source, source + steps) for source in range(leading, last)])


def for_sending(shard):

    def short(part):
        return part.astype(jnp.bfloat16) if part.dtype == jnp.float32 else part

    return jax.tree.map(short, shard)


def attend(carry, grouped, block_rows, visible):
    biggest, totals, accum = carry
    count = block_rows.shape[0]
    half = block_rows.shape[1] // 2
    keys_part = block_rows[:, :half].reshape(count, KVH, HD)
    values_part = block_rows[:, half:].reshape(count, KVH, HD)
    scores = jnp.einsum(
        "qhgd,khd->hgqk", grouped, keys_part, preferred_element_type=jnp.float32
    ) * (1.0 / math.sqrt(HD))
    masked = jnp.where(visible[None, None], scores, NEG)
    renewed = jnp.maximum(biggest, jnp.max(masked, axis=-1))
    weights = jnp.where(visible[None, None], jnp.exp(scores - renewed[..., None]), 0.0)
    factor = jnp.exp(biggest - renewed)
    totals = totals * factor + jnp.sum(weights, axis=-1)
    accum = accum * factor[..., None] + jnp.einsum(
        "hgqk,khd->hgqd",
        weights.astype(jnp.bfloat16),
        values_part,
        preferred_element_type=jnp.float32,
    )
    return (renewed, totals, accum)


def fetch_pages(owner_list, slot_list, pool_pages, capacity):
    owners_count = lax.axis_size("cache")
    onehot = (owner_list[:, None] == jnp.arange(owners_count, dtype=jnp.int32)[None, :]).astype(
        jnp.int32
    )
    earlier = jnp.cumsum(onehot, axis=0) - onehot
    ranking = jnp.sum(earlier * onehot, axis=1)
    wanted_slots = (
        jnp.zeros((owners_count, capacity), jnp.int32).at[owner_list, ranking].set(slot_list)
    )
    arrived = lax.all_to_all(
        pool_pages[lax.all_to_all(wanted_slots, "cache", split_axis=0, concat_axis=0, tiled=True)],
        "cache",
        split_axis=0,
        concat_axis=0,
        tiled=True,
    )
    return arrived[owner_list, ranking]


def combine(earlier, later):
    return (earlier[0] * later[0], later[0][:, None, None] * earlier[1] + later[1])


def local(
    queries,
    kv_new,
    page_pool,
    page_owner,
    page_slot,
    prefix_len,
    suffix_len,
    ssm_in,
    b_in,
    c_in,
    step_size,
    decay_rate,
    skip_gain,
    prior_state,
):
    blocks = lax.axis_size("blk")
    position_here = lax.axis_index("blk")
    tokens = queries.shape[1]
    kv_width = kv_new.shape[2]
    group = QH // KVH
    prefix_limit = prefix_len[0]
    suffix_limit = suffix_len[0]
    local_positions = jnp.arange(tokens, dtype=jnp.int32)
    query_positions = position_here * tokens + local_positions
    grouped = queries[0].reshape(tokens, KVH, group, HD)
    carry = (
        jnp.full((KVH, group, tokens), NEG, jnp.float32),
        jnp.zeros((KVH, group, tokens), jnp.float32),
        jnp.zeros((KVH, group, tokens, HD), jnp.float32),
    )
    pool_pages = page_pool[0]
    capacity = max(2, 2 * LIST // lax.axis_size("cache"))
    all_owners, all_slots = (
        lax.all_gather(page_owner[:, :, :, 0], "blk", axis=1, tiled=True),
        lax.all_gather(page_slot, "blk", axis=1, tiled=True),
    )
    fetched = fetch_pages(
        all_owners[0].reshape(-1), all_slots[0].reshape(-1), pool_pages, capacity * blocks
    )
    page_rows = fetched.reshape(-1, kv_width)
    block_ids = jnp.arange(blocks, dtype=jnp.int32)[:, None, None]
    item_ids = jnp.arange(LIST, dtype=jnp.int32)[None, :, None]
    offsets = jnp.arange(PAGE, dtype=jnp.int32)[None, None, :]
    page_positions = ((item_ids * blocks + block_ids) * PAGE + offsets).reshape(-1)
    valid = page_positions < prefix_limit
    total = page_rows.shape[0]
    width = 512

    def page_block(index, state):
        rows_block = lax.dynamic_slice_in_dim(page_rows, index * width, width, 0)
        seen = lax.dynamic_slice_in_dim(valid, index * width, width, 0)
        return attend(state, grouped, rows_block, jnp.broadcast_to(seen[None, :], (tokens, width)))

    carry = lax.fori_loop(0, total // width, page_block, carry)
    suffix_rows = kv_new[0]
    for step in range(blocks):
        if step > 0:
            suffix_rows = passed_along(suffix_rows, "blk", 1)
        anchor = (position_here - step) % blocks
        key_positions = anchor * tokens + local_positions
        carry = attend(
            carry,
            grouped,
            suffix_rows,
            (key_positions[None, :] <= query_positions[:, None])
            & (key_positions[None, :] < suffix_limit),
        )
    biggest, totals, accum = carry
    mixed = jnp.transpose(accum / totals[..., None], (2, 0, 1, 3)).reshape(tokens, QH * HD)
    attn_out = jnp.where((query_positions < suffix_limit)[:, None], mixed, 0.0).astype(
        jnp.bfloat16
    )[None]
    inputs = ssm_in[0].reshape(tokens, SH, HP)
    b_rows = b_in[0]
    c_rows = c_in[0]
    steps_dt = step_size[0]
    logs = jnp.cumsum(-steps_dt * decay_rate[None, :], axis=0)
    last = logs[-1]
    gram = jnp.dot(c_rows, b_rows.T, preferred_element_type=jnp.float32)
    lower = local_positions[:, None] >= local_positions[None, :]
    exponent = jnp.where(lower[None], logs.T[:, :, None] - logs.T[:, None, :], NEG)
    mixing = (gram[None] * jnp.exp(exponent) * steps_dt.T[:, None, :]).astype(jnp.bfloat16)
    inner = jnp.einsum("hts,shp->thp", mixing, inputs, preferred_element_type=jnp.float32)
    scaled = (
        (jnp.exp(last[None, :] - logs) * steps_dt)[:, :, None] * inputs.astype(jnp.float32)
    ).astype(jnp.bfloat16)
    local_state = jnp.einsum("shp,sn->hpn", scaled, b_rows, preferred_element_type=jnp.float32)
    local_decay = jnp.exp(last)
    identity = (jnp.ones((SH,), jnp.float32), jnp.zeros((SH, HP, NS), jnp.float32))
    prefix_decay, prefix_state = identity
    for round_index in range(blocks - 1):
        outgoing = combine((prefix_decay, prefix_state), (local_decay, local_state))
        incoming = passed_along((for_sending(outgoing[0]), for_sending(outgoing[1])), "blk", 1)
        prefix_decay = jnp.where(position_here == 0, identity[0], incoming[0])
        prefix_state = jnp.where(position_here == 0, identity[1], incoming[1])
    entering = prefix_decay[:, None, None] * prior_state[0] + prefix_state
    carried = jnp.exp(logs)[:, :, None] * jnp.einsum(
        "tn,hpn->thp", c_rows.astype(jnp.float32), entering, precision=lax.Precision.HIGHEST
    )
    result = inner + carried + skip_gain[None, :, None] * inputs.astype(jnp.float32)
    result = jnp.where((query_positions < suffix_limit)[:, None, None], result, 0.0)
    ssm_out = result.reshape(tokens, SH * HP).astype(jnp.bfloat16)[None]
    return (attn_out, ssm_out)


def solution(mesh):
    in_specs = (
        P(("groups", "cache"), "blk", None),
        P(("groups", "cache"), "blk", None),
        P(("groups", "cache"), None, None, None),
        P(("groups", "cache"), "blk", None, None),
        P(("groups", "cache"), "blk", None),
        P(("groups", "cache")),
        P(("groups", "cache")),
        P(("groups", "cache"), "blk", None),
        P(("groups", "cache"), "blk", None),
        P(("groups", "cache"), "blk", None),
        P(("groups", "cache"), "blk", None),
        P(),
        P(),
        P(("groups", "cache"), None, None, None),
    )
    out_specs = (P(("groups", "cache"), "blk", None), P(("groups", "cache"), "blk", None))
    return jax.shard_map(local, mesh=mesh, in_specs=in_specs, out_specs=out_specs, check_vma=False)
```

profile of v0, /device:TPU:0, one launch (start us, length us, event | category | flops | bytes accessed | tf_op | source)
XLA Modules:
  0.0 198.7 jit_solution(4039296911272048753)
XLA Ops:
  0.6 6.3 %all-gather = s32[1,4,32,1]{2,3,0,1:T(1,128)S(1)} all-gather(s32[1,1,32,1]{2,3,0,1:T(1,128)} %bitcast.279), channel_id=2, replica_groups=mesh['groups'=2,'cache'=4,'blk'=4] {'blk'}, dimensions={1}, use_global_device_ids=true | all-gather | bytes 640 | tf_op jit(solution)/shard_map/all_gather | solution.py:113
  8.7 5.4 %all_gather.7 = s32[1,4,32]{2,0,1:T(1,128)S(1)} all-gather(s32[1,1,32]{2,0,1:T(1,128)} %bitcast.280), channel_id=1, replica_groups=mesh['groups'=2,'cache'=4,'blk'=4] {'blk'}, dimensions={1}, use_global_device_ids=true | all-gather | bytes 640 | tf_op jit(solution)/shard_map/all_gather | solution.py:114
  15.4 19.7 %scatter_fusion = s32[4,64]{1,0:T(4,128)} fusion(s32[4,64]{1,0:T(4,128)} %broadcast.351, s32[128]{0:T(128)S(1)} %get-tuple-element.209, s32[128]{0:T(128)S(1)} %reshape.502), kind=kCustom, calls=%fused_computation.2 | custom fusion | bytes 2560 | tf_op jit(solution)/shard_map/scatter | solution.py:63
  35.1 5.1 %all-to-all-start = ((s32[4,1,64]{2,1,0:T(1,128)}), s32[4,1,64]{2,1,0:T(1,128)S(1)}, u32[]{:S(2)}, u32[]{:S(2)}) async-start(s32[4,1,64]{2,1,0:T(1,128)} %bitcast.8), calls=%async_computation | async-start | bytes 4096 | tf_op jit(solution)/shard_map/all_to_all | solution.py:66
  40.3 1.1 copy.103
  41.4 2.6 %collective-permute-start = (bf16[128,1024]{0,1:T(8,128)(2,1)S(1)}, bf16[128,1024]{0,1:T(8,128)(2,1)}, u32[]{:S(2)}, u32[]{:S(2)}) collective-permute-start(bf16[128,1024]{0,1:T(8,128)(2,1)S(1)} %bitcast.243), channel_id=1, source_target_pairs={{0,1},{1,2},{2,3},{4,5},{5,6},{6,7},{8,9},{9,10},{10,11},{12,13},{... | collective-permute-start | bytes 786440 | tf_op jit(solution)/shard_map/ppermute | solution.py:21
  46.3 3.3 %collective-permute-start.3 = (bf16[32]{0:T(256)(128)(2,1)}, bf16[32]{0:T(256)(128)(2,1)}, u32[]{:S(2)}, u32[]{:S(2)}) collective-permute-start(bf16[32]{0:T(256)(128)(2,1)} %fusion.89), channel_id=1, source_target_pairs={{0,1},{1,2},{2,3},{4,5},{5,6},{6,7},{8,9},{9,10},{10,11},{12,13},{... | collective-permute-start | bytes 200 | tf_op jit(solution)/shard_map/ppermute | solution.py:21
  49.7 2.8 %gather_fusion = bf16[256,8,1024]{2,1,0:T(8,128)(2,1)} fusion(bf16[128,8,1024]{2,1,0:T(8,128)(2,1)S(1)} %bitcast.226, s32[1024]{0:T(1024)S(1)} %pad_clamp_fusion), kind=kCustom, calls=%fused_computation | custom fusion | bytes 8389632 | tf_op jit(solution)/shard_map/gather | solution.py:66
  52.5 5.2 %all-to-all-start.1 = ((bf16[4,64,8,1024]{3,2,1,0:T(8,128)(2,1)}), bf16[4,64,8,1024]{3,2,1,0:T(8,128)(2,1)}, u32[]{:S(2)}, u32[]{:S(2)}) async-start(bf16[4,64,8,1024]{3,2,1,0:T(8,128)(2,1)} %bitcast.234), calls=%async_computation.1 | async-start | bytes 8388608 | tf_op jit(solution)/shard_map/all_to_all | solution.py:65
  59.8 1.3 copy.122
  65.7 2.7 %convolution_bitcast_fusion.1 = f32[128,32,64]{0,2,1:T(8,128)} fusion(bf16[128,32,64]{0,2,1:T(8,128)(2,1)S(1)} %bitcast.237, f32[32,128]{1,0:T(8,128)} %bitcast.276, f32[32,128]{1,0:T(8,128)} %copy.119, f32[128,128]{1,0:T(8,128)S(1)} %fusion.73, pred[128,128]{1,0:T(8,128)(4,1)S(1)} %iota_compare_fusion), kind=kOutput, calls=%fused_computation.46 | convolution fusion | flops 69730304 | bytes 1687552 | tf_op jit(solution)/shard_map/hts,shp->thp/dot_general | solution.py:162
  68.4 2.0 %select_reduce_fusion.3 = (f32[4,4,128]{2,1,0:T(4,128)}, f32[4,4,128,128]{2,3,1,0:T(8,128)}) fusion(pred[128,128]{0,1:T(8,128)(4,1)S(1)} %get-tuple-element.228, bf16[128,4,128,1]{0,2,3,1:T(8,128)(2,1)S(1)} %bitcast.251, bf16[128,4,4,128]{0,3,2,1:T(8,128)(2,1)S(1)} %bitcast.229), kind=kOutput, calls=%fused_computation.70 | convolution fusion | flops 67893248 | bytes 1728512 | tf_op jit(solution)/shard_map/qhgd,khd->hgqk/dot_general | solution.py:38
  71.9 1.3 collective-permute-start.4
  74.0 1.4 add_convert_fusion.2
  75.5 3.0 %collective-permute-start.6 = (bf16[32,64,128]{2,1,0:T(8,128)(2,1)}, bf16[32,64,128]{2,1,0:T(8,128)(2,1)}, u32[]{:S(2)}, u32[]{:S(2)}) collective-permute-start(bf16[32,64,128]{2,1,0:T(8,128)(2,1)} %get-tuple-element.240), channel_id=1, source_target_pairs={{0,1},{1,2},{2,3},{4,5},{5,6},{6,7},{8,9},{9,10},{10,11},{12,13},{... | collective-permute-start | bytes 1572872 | tf_op jit(solution)/shard_map/ppermute | solution.py:21
  78.6 1.0 copy.102
  80.3 3.1 %collective-permute-start.5 = (bf16[32]{0:T(256)(128)(2,1)S(1)}, bf16[32]{0:T(256)(128)(2,1)S(1)}, u32[]{:S(2)}, u32[]{:S(2)}) collective-permute-start(bf16[32]{0:T(256)(128)(2,1)S(1)} %get-tuple-element.225), channel_id=1, source_target_pairs={{0,1},{1,2},{2,3},{4,5},{5,6},{6,7},{8,9},{9,10},{10,11},{12,13},{... | collective-permute-start | bytes 200 | tf_op jit(solution)/shard_map/ppermute | solution.py:21
  83.4 1.5 copy.123
  85.0 3.1 %collective-permute-start.1 = (bf16[128,1024]{0,1:T(8,128)(2,1)}, bf16[128,1024]{0,1:T(8,128)(2,1)S(1)}, u32[]{:S(2)}, u32[]{:S(2)}) collective-permute-start(bf16[128,1024]{0,1:T(8,128)(2,1)} %collective-permute-done), channel_id=1, source_target_pairs={{0,1},{1,2},{2,3},{4,5},{5,6},{6,7},{8,9},{9,10},{10,11},{12,13},{... | collective-permute-start | bytes 786440 | tf_op jit(solution)/shard_map/ppermute | solution.py:21
  88.0 1.6 add_convert_fusion.1
  89.6 4.4 %collective-permute-start.7 = (bf16[32,64,128]{2,1,0:T(8,128)(2,1)S(1)}, bf16[32,64,128]{2,1,0:T(8,128)(2,1)S(1)}, u32[]{:S(2)}, u32[]{:S(2)}) collective-permute-start(bf16[32,64,128]{2,1,0:T(8,128)(2,1)S(1)} %add_convert_fusion.1), channel_id=1, source_target_pairs={{0,1},{1,2},{2,3},{4,5},{5,6},{6,7},{8,9},{9,10},{10,11},{12,13},{... | collective-permute-start | bytes 1572872 | tf_op jit(solution)/shard_map/ppermute | solution.py:21
  94.0 1.0 fusion.95
  95.1 1.9 select_reduce_fusion.2
  97.0 1.9 collective-permute-start.2
  99.8 3.2 %collective-permute-start.8 = (bf16[32,64,128]{2,1,0:T(8,128)(2,1)S(1)}, bf16[32,64,128]{2,1,0:T(8,128)(2,1)S(1)}, u32[]{:S(2)}, u32[]{:S(2)}) collective-permute-start(bf16[32,64,128]{2,1,0:T(8,128)(2,1)S(1)} %add_convert_fusion), channel_id=1, source_target_pairs={{0,1},{1,2},{2,3},{4,5},{5,6},{6,7},{8,9},{9,10},{10,11},{12,13},{... | collective-permute-start | bytes 1572872 | tf_op jit(solution)/shard_map/ppermute | solution.py:21
  103.0 2.6 %select_reduce_fusion.1 = (f32[4,4,128]{2,1,0:T(4,128)}, f32[4,4,128,128]{2,3,1,0:T(8,128)}) fusion(pred[128,128]{0,1:T(8,128)(4,1)} %get-tuple-element.229, bf16[128,4,128,1]{0,2,3,1:T(8,128)(2,1)S(1)} %bitcast.250, bf16[128,4,4,128]{0,3,2,1:T(8,128)(2,1)S(1)} %bitcast.232), kind=kOutput, calls=%fused_computation.66 | convolution fusion | flops 67893248 | bytes 1728512 | tf_op jit(solution)/shard_map/qhgd,khd->hgqk/dot_general | solution.py:38
  106.4 2.0 select_reduce_fusion
  109.3 1.0 copy.126
  110.3 40.6 %all-to-all-done.1 = bf16[4,64,8,1024]{3,2,1,0:T(8,128)(2,1)} async-done(((bf16[4,64,8,1024]{3,2,1,0:T(8,128)(2,1)}), bf16[4,64,8,1024]{3,2,1,0:T(8,128)(2,1)}, u32[]{:S(2)}, u32[]{:S(2)}) %all-to-all-start.1) | async-done | bytes 4194336 | tf_op jit(solution)/shard_map/all_to_all | solution.py:65
  150.9 4.4 %gather_fusion.1 = bf16[128,8,1024]{2,1,0:T(8,128)(2,1)} fusion(bf16[4,64,8,1024]{3,2,1,0:T(8,128)(2,1)} %all-to-all-done.1, s32[128]{0:T(128)S(1)} %bitcast.236), kind=kCustom, calls=%fused_computation.1 | custom fusion | bytes 4195328 | tf_op jit(solution)/shard_map/gather | solution.py:72
  155.3 31.0 %while.18 = (s32[]{:T(128)}, f32[4,4,128]{2,1,0:T(4,128)S(1)}, f32[4,4,128]{2,1,0:T(4,128)}, f32[4,4,128,128]{3,2,1,0:T(8,128)}, pred[1024]{0:T(1024)(128)(4,1)S...) while((s32[]{:T(128)}, f32[4,4,128]{2,1,0:T(4,128)S(1)}, ...), condition=%wide.region_6.7_spmd.clone, body=%wide.region_3.6_spmd.clone.sunk | while | flops 549201920 | bytes 20581072 | solution.py:133
  155.4 1.3 fusion.128
  156.7 1.1 copy.164
  157.7 4.2 %fusion.129 = (f32[4,4,128]{2,1,0:T(4,128)S(1)}, f32[4,512,128,4]{2,1,3,0:T(8,128)}) fusion(pred[512]{0:T(512)(128)(4,1)S(1)} %dynamic_slice.17, bf16[512,4,128,1]{0,2,3,1:T(8,128)(2,1)} %bitcast.227, bf16[128,4,4,128]{3,0,2,1:T(8,128)(2,1)} %get-tuple-element.344), kind=kOutput, calls=%fused_computation.5.clone.1 | convolution fusion | flops 271579136 | bytes 5251584 | tf_op jit(solution)/shard_map/while/body/eval_jaxpr/qhgd,khd->hgqk/dot_general | solution.py:38
  161.9 3.1 %fusion.130 = f32[4,4,128]{2,1,0:T(4,128)S(1)} fusion(f32[4,512,128,4]{2,1,3,0:T(8,128)} %get-tuple-element.310, f32[4,4,128]{2,1,0:T(4,128)S(1)} %select_maximum_fusion.2, pred[512]{0:T(512)(128)(4,1)S(1)} %dynamic_slice.17), kind=kLoop, calls=%fused_computation.9.clone.1 | loop fusion | flops 4192256 | bytes 4211200 | tf_op jit(solution)/shard_map/while/body/eval_jaxpr/reduce_sum | solution.py:45
  165.8 4.5 %fusion.132 = f32[4,4,128,128]{3,2,1,0:T(8,128)} fusion(bf16[512,4,128,1]{0,2,3,1:T(8,128)(2,1)S(1)} %bitcast.235, f32[4,512,128,4]{2,1,3,0:T(8,128)} %get-tuple-element.310, f32[4,4,128]{2,1,0:T(4,128)S(1)} %select_maximum_fusion.2, pred[512]{0:T(512)(128)(4,1)S(1)} %dynamic_slice.17, f32[4,4,128,128]{3,2,1,0:T(8,128)} %get-tuple-element.329, ...), kind=kOutput, calls=%fused_computation.15.clone.1 | convolution fusion | flops 273416192 | bytes 6832641 | tf_op jit(solution)/shard_map/while/body/eval_jaxpr/hgqk,khd->hgqd/dot_general | solution.py:46
  170.4 1.3 fusion.128
  171.7 1.1 copy.164
  172.7 4.2 %fusion.129 = (f32[4,4,128]{2,1,0:T(4,128)S(1)}, f32[4,512,128,4]{2,1,3,0:T(8,128)}) fusion(pred[512]{0:T(512)(128)(4,1)S(1)} %dynamic_slice.17, bf16[512,4,128,1]{0,2,3,1:T(8,128)(2,1)} %bitcast.227, bf16[128,4,4,128]{3,0,2,1:T(8,128)(2,1)} %get-tuple-element.344), kind=kOutput, calls=%fused_computation.5.clone.1 | convolution fusion | flops 271579136 | bytes 5251584 | tf_op jit(solution)/shard_map/while/body/eval_jaxpr/qhgd,khd->hgqk/dot_general | solution.py:38
  176.9 3.1 %fusion.130 = f32[4,4,128]{2,1,0:T(4,128)S(1)} fusion(f32[4,512,128,4]{2,1,3,0:T(8,128)} %get-tuple-element.310, f32[4,4,128]{2,1,0:T(4,128)S(1)} %select_maximum_fusion.2, pred[512]{0:T(512)(128)(4,1)S(1)} %dynamic_slice.17), kind=kLoop, calls=%fused_computation.9.clone.1 | loop fusion | flops 4192256 | bytes 4211200 | tf_op jit(solution)/shard_map/while/body/eval_jaxpr/reduce_sum | solution.py:45
  180.0 1.3 fusion.131
  181.5 4.8 %fusion.132 = f32[4,4,128,128]{3,2,1,0:T(8,128)} fusion(bf16[512,4,128,1]{0,2,3,1:T(8,128)(2,1)S(1)} %bitcast.235, f32[4,512,128,4]{2,1,3,0:T(8,128)} %get-tuple-element.310, f32[4,4,128]{2,1,0:T(4,128)S(1)} %select_maximum_fusion.2, pred[512]{0:T(512)(128)(4,1)S(1)} %dynamic_slice.17, f32[4,4,128,128]{3,2,1,0:T(8,128)} %get-tuple-element.329, ...), kind=kOutput, calls=%fused_computation.15.clone.1 | convolution fusion | flops 273416192 | bytes 6832641 | tf_op jit(solution)/shard_map/while/body/eval_jaxpr/hgqk,khd->hgqd/dot_general | solution.py:46
  186.3 2.7 %copy.106 = f32[4,4,128,128]{2,3,1,0:T(8,128)} copy(f32[4,4,128,128]{3,2,1,0:T(8,128)} %get-tuple-element.128) | data formatting | bytes 2097152 | tf_op jit(solution)/shard_map/while | solution.py:133
  189.9 1.4 fusion.47
  191.3 1.4 fusion.45
  192.8 1.4 fusion.43
  194.2 1.0 fusion.41
  197.8 1.0 select_convert_fusion
  (128 shorter events, 20.8 us)
Async XLA Ops:
  0.6 49.0 %copy-start = (bf16[1,128,8,1024]{3,2,1,0:T(8,128)(2,1)S(1)}, bf16[1,128,8,1024]{3,2,1,0:T(8,128)(2,1)}, u32[]{:S(2)}) copy-start(bf16[1,128,8,1024]{3,2,1,0:T(8,128)(2,1)} %param.18) | copy-start | bytes 6291460
  35.1 14.4 %all-to-all-start = ((s32[4,1,64]{2,1,0:T(1,128)}), s32[4,1,64]{2,1,0:T(1,128)S(1)}, u32[]{:S(2)}, u32[]{:S(2)}) async-start(s32[4,1,64]{2,1,0:T(1,128)} %bitcast.8), calls=%async_computation | async-start | bytes 4096 | tf_op jit(solution)/shard_map/all_to_all | solution.py:66
  41.4 43.6 %collective-permute-start = (bf16[128,1024]{0,1:T(8,128)(2,1)S(1)}, bf16[128,1024]{0,1:T(8,128)(2,1)}, u32[]{:S(2)}, u32[]{:S(2)}) collective-permute-start(bf16[128,1024]{0,1:T(8,128)(2,1)S(1)} %bitcast.243), channel_id=1, source_target_pairs={{0,1},{1,2},{2,3},{4,5},{5,6},{6,7},{8,9},{9,10},{10,11},{12,13},{... | collective-permute-start | bytes 786440 | tf_op jit(solution)/shard_map/ppermute | solution.py:21
  46.3 25.0 %collective-permute-start.3 = (bf16[32]{0:T(256)(128)(2,1)}, bf16[32]{0:T(256)(128)(2,1)}, u32[]{:S(2)}, u32[]{:S(2)}) collective-permute-start(bf16[32]{0:T(256)(128)(2,1)} %fusion.89), channel_id=1, source_target_pairs={{0,1},{1,2},{2,3},{4,5},{5,6},{6,7},{8,9},{9,10},{10,11},{12,13},{... | collective-permute-start | bytes 200 | tf_op jit(solution)/shard_map/ppermute | solution.py:21
  52.5 6.4 %copy-start.9 = (bf16[1,128,2048]{2,1,0:T(8,128)(2,1)S(1)}, bf16[1,128,2048]{2,1,0:T(8,128)(2,1)}, u32[]{:S(2)}) copy-start(bf16[1,128,2048]{2,1,0:T(8,128)(2,1)} %param.16) | copy-start | bytes 1572868
  52.5 98.4 %all-to-all-start.1 = ((bf16[4,64,8,1024]{3,2,1,0:T(8,128)(2,1)}), bf16[4,64,8,1024]{3,2,1,0:T(8,128)(2,1)}, u32[]{:S(2)}, u32[]{:S(2)}) async-start(bf16[4,64,8,1024]{3,2,1,0:T(8,128)(2,1)} %bitcast.234), calls=%async_computation.1 | async-start | bytes 8388608 | tf_op jit(solution)/shard_map/all_to_all | solution.py:65
  63.4 7.0 %copy-start.14 = (pred[128,128]{0,1:T(8,128)(4,1)}, pred[128,128]{0,1:T(8,128)(4,1)S(1)}, u32[]{:S(2)}) copy-start(pred[128,128]{0,1:T(8,128)(4,1)S(1)} %get-tuple-element.228) | copy-start | bytes 49156
  65.0 9.0 %copy-start.18 = (bf16[1,128,128]{2,1,0:T(8,128)(2,1)S(1)}, bf16[1,128,128]{2,1,0:T(8,128)(2,1)}, u32[]{:S(2)}) copy-start(bf16[1,128,128]{2,1,0:T(8,128)(2,1)} %param.24) | copy-start | bytes 98308
  68.4 26.7 %copy-start.12 = (pred[128,128]{0,1:T(8,128)(4,1)S(1)}, pred[128,128]{0,1:T(8,128)(4,1)}, u32[]{:S(2)}) copy-start(pred[128,128]{0,1:T(8,128)(4,1)} %get-tuple-element.231) | copy-start | bytes 49156
  71.9 2.1 %collective-permute-start.4 = (bf16[32]{0:T(256)(128)(2,1)S(1)}, bf16[32]{0:T(256)(128)(2,1)S(1)}, u32[]{:S(2)}, u32[]{:S(2)}) collective-permute-start(bf16[32]{0:T(256)(128)(2,1)S(1)} %fusion.78), channel_id=1, source_target_pairs={{0,1},{1,2},{2,3},{4,5},{5,6},{6,7},{8,9},{9,10},{10,11},{12,13},{... | collective-permute-start | bytes 200 | tf_op jit(solution)/shard_map/ppermute | solution.py:21
  74.0 23.0 %copy-start.22 = (f32[32]{0:T(128)}, f32[32]{0:T(128)S(1)}, u32[]{:S(2)}) copy-start(f32[32]{0:T(128)S(1)} %get-tuple-element.227) | copy-start | bytes 388
  75.5 12.6 %collective-permute-start.6 = (bf16[32,64,128]{2,1,0:T(8,128)(2,1)}, bf16[32,64,128]{2,1,0:T(8,128)(2,1)}, u32[]{:S(2)}, u32[]{:S(2)}) collective-permute-start(bf16[32,64,128]{2,1,0:T(8,128)(2,1)} %get-tuple-element.240), channel_id=1, source_target_pairs={{0,1},{1,2},{2,3},{4,5},{5,6},{6,7},{8,9},{9,10},{10,11},{12,13},{... | collective-permute-start | bytes 1572872 | tf_op jit(solution)/shard_map/ppermute | solution.py:21
  78.6 29.7 %copy-start.23 = (pred[128]{0:T(512)(128)(4,1)}, pred[128]{0:T(512)(128)(4,1)S(1)}, u32[]{:S(2)}) copy-start(pred[128]{0:T(512)(128)(4,1)S(1)} %broadcast_compare_fusion.4) | copy-start | bytes 388
  80.3 4.6 %collective-permute-start.5 = (bf16[32]{0:T(256)(128)(2,1)S(1)}, bf16[32]{0:T(256)(128)(2,1)S(1)}, u32[]{:S(2)}, u32[]{:S(2)}) collective-permute-start(bf16[32]{0:T(256)(128)(2,1)S(1)} %get-tuple-element.225), channel_id=1, source_target_pairs={{0,1},{1,2},{2,3},{4,5},{5,6},{6,7},{8,9},{9,10},{10,11},{12,13},{... | collective-permute-start | bytes 200 | tf_op jit(solution)/shard_map/ppermute | solution.py:21
  84.9 14.0 %copy-start.4 = (f32[32,64,128]{2,1,0:T(8,128)S(1)}, f32[32,64,128]{2,1,0:T(8,128)}, u32[]{:S(2)}) copy-start(f32[32,64,128]{2,1,0:T(8,128)} %get-tuple-element.241) | copy-start | bytes 3145732
  85.0 12.1 %collective-permute-start.1 = (bf16[128,1024]{0,1:T(8,128)(2,1)}, bf16[128,1024]{0,1:T(8,128)(2,1)S(1)}, u32[]{:S(2)}, u32[]{:S(2)}) collective-permute-start(bf16[128,1024]{0,1:T(8,128)(2,1)} %collective-permute-done), channel_id=1, source_target_pairs={{0,1},{1,2},{2,3},{4,5},{5,6},{6,7},{8,9},{9,10},{10,11},{12,13},{... | collective-permute-start | bytes 786440 | tf_op jit(solution)/shard_map/ppermute | solution.py:21
  88.0 18.3 %copy-start.16 = (pred[128,128]{0,1:T(8,128)(4,1)S(1)}, pred[128,128]{0,1:T(8,128)(4,1)}, u32[]{:S(2)}) copy-start(pred[128,128]{0,1:T(8,128)(4,1)} %get-tuple-element.230) | copy-start | bytes 49156
  89.6 9.4 %collective-permute-start.7 = (bf16[32,64,128]{2,1,0:T(8,128)(2,1)S(1)}, bf16[32,64,128]{2,1,0:T(8,128)(2,1)S(1)}, u32[]{:S(2)}, u32[]{:S(2)}) collective-permute-start(bf16[32,64,128]{2,1,0:T(8,128)(2,1)S(1)} %add_convert_fusion.1), channel_id=1, source_target_pairs={{0,1},{1,2},{2,3},{4,5},{5,6},{6,7},{8,9},{9,10},{10,11},{12,13},{... | collective-permute-start | bytes 1572872 | tf_op jit(solution)/shard_map/ppermute | solution.py:21
  95.0 13.3 %copy-start.7 = (f32[1,32,64,128]{3,2,1,0:T(8,128)S(1)}, f32[1,32,64,128]{3,2,1,0:T(8,128)}, u32[]{:S(2)}) copy-start(f32[1,32,64,128]{3,2,1,0:T(8,128)} %param.29) | copy-start | bytes 3145732
  95.0 13.3 %copy-start.8 = (f32[128,32,64]{0,2,1:T(8,128)S(1)}, f32[128,32,64]{0,2,1:T(8,128)}, u32[]{:S(2)}) copy-start(f32[128,32,64]{0,2,1:T(8,128)} %convolution_bitcast_fusion.1) | copy-start | bytes 3145732
  95.0 13.3 %copy-start.19 = (bf16[1,128,128]{2,1,0:T(8,128)(2,1)S(1)}, bf16[1,128,128]{2,1,0:T(8,128)(2,1)}, u32[]{:S(2)}) copy-start(bf16[1,128,128]{2,1,0:T(8,128)(2,1)} %param.25) | copy-start | bytes 98308
  95.1 13.3 %copy-start.21 = (f32[128,32]{0,1:T(8,128)S(1)}, f32[128,32]{0,1:T(8,128)}, u32[]{:S(2)}) copy-start(f32[128,32]{0,1:T(8,128)} %copy.123) | copy-start | bytes 49156
  95.1 13.3 %copy-start.26 = (f32[32]{0:T(128)S(1)}, f32[32]{0:T(128)}, u32[]{:S(2)}) copy-start(f32[32]{0:T(128)} %param.28) | copy-start | bytes 388
  97.0 8.6 %collective-permute-start.2 = (bf16[128,1024]{0,1:T(8,128)(2,1)S(1)}, bf16[128,1024]{0,1:T(8,128)(2,1)S(1)}, u32[]{:S(2)}, u32[]{:S(2)}) collective-permute-start(bf16[128,1024]{0,1:T(8,128)(2,1)S(1)} %collective-permute-done.1), channel_id=1, source_target_pairs={{0,1},{1,2},{2,3},{4,5},{5,6},{6,7},{8,9},{9,10},{10,11},{12,13},{... | collective-permute-start | bytes 786440 | tf_op jit(solution)/shard_map/ppermute | solution.py:21
  99.8 8.6 %collective-permute-start.8 = (bf16[32,64,128]{2,1,0:T(8,128)(2,1)S(1)}, bf16[32,64,128]{2,1,0:T(8,128)(2,1)S(1)}, u32[]{:S(2)}, u32[]{:S(2)}) collective-permute-start(bf16[32,64,128]{2,1,0:T(8,128)(2,1)S(1)} %add_convert_fusion), channel_id=1, source_target_pairs={{0,1},{1,2},{2,3},{4,5},{5,6},{6,7},{8,9},{9,10},{10,11},{12,13},{... | collective-permute-start | bytes 1572872 | tf_op jit(solution)/shard_map/ppermute | solution.py:21
  108.3 47.0 %copy-start.25 = (pred[1024]{0:T(1024)(128)(4,1)S(1)}, pred[1024]{0:T(1024)(128)(4,1)}, u32[]{:S(2)}) copy-start(pred[1024]{0:T(1024)(128)(4,1)} %lt.128) | copy-start | bytes 3076
  186.3 7.9 %copy-start.1 = (f32[4,4,128,128]{2,3,1,0:T(8,128)S(1)}, f32[4,4,128,128]{2,3,1,0:T(8,128)}, u32[]{:S(2)}) copy-start(f32[4,4,128,128]{2,3,1,0:T(8,128)} %get-tuple-element.239) | copy-start | bytes 3145732
  186.3 9.7 %copy-start.10 = (bf16[128,512]{0,1:T(8,128)(2,1)S(1)}, bf16[128,512]{0,1:T(8,128)(2,1)}, u32[]{:S(2)}) copy-start(bf16[128,512]{0,1:T(8,128)(2,1)} %get-tuple-element.222) | copy-start | bytes 393220
  189.0 7.0 %copy-start.5 = (f32[4,4,128,128]{2,3,1,0:T(8,128)S(1)}, f32[4,4,128,128]{2,3,1,0:T(8,128)}, u32[]{:S(2)}) copy-start(f32[4,4,128,128]{2,3,1,0:T(8,128)} %copy.106) | copy-start | bytes 3145732
  189.0 7.0 %copy-start.15 = (pred[128,128]{0,1:T(8,128)(4,1)S(1)}, pred[128,128]{0,1:T(8,128)(4,1)}, u32[]{:S(2)}) copy-start(pred[128,128]{0,1:T(8,128)(4,1)} %copy-done.14) | copy-start | bytes 49156
  189.0 7.3 %copy-start.2 = (f32[4,4,128,128]{2,3,1,0:T(8,128)S(1)}, f32[4,4,128,128]{2,3,1,0:T(8,128)}, u32[]{:S(2)}) copy-start(f32[4,4,128,128]{2,3,1,0:T(8,128)} %get-tuple-element.237) | copy-start | bytes 3145732
  189.0 7.4 %copy-start.13 = (pred[128,128]{0,1:T(8,128)(4,1)S(1)}, pred[128,128]{0,1:T(8,128)(4,1)}, u32[]{:S(2)}) copy-start(pred[128,128]{0,1:T(8,128)(4,1)} %get-tuple-element.231) | copy-start | bytes 49156
  194.2 2.5 %copy-start.3 = (f32[4,4,128,128]{2,3,1,0:T(8,128)S(1)}, f32[4,4,128,128]{2,3,1,0:T(8,128)}, u32[]{:S(2)}) copy-start(f32[4,4,128,128]{2,3,1,0:T(8,128)} %get-tuple-element.235) | copy-start | bytes 3145732
  194.2 2.5 %copy-start.11 = (pred[128,128]{0,1:T(8,128)(4,1)S(1)}, pred[128,128]{0,1:T(8,128)(4,1)}, u32[]{:S(2)}) copy-start(pred[128,128]{0,1:T(8,128)(4,1)} %get-tuple-element.229) | copy-start | bytes 49156
  196.0 1.2 copy-start.6
  196.0 1.2 copy-start.17
  196.0 1.2 copy-start.20
  196.7 1.1 copy-start.24
where the time goes:
time: 201 us; the launch traced here: 199 us
  local copies, waits for them, and re-layouts  48.4 us (24%)
  waiting for transfers between devices  41.3 us (21%)
  starting transfers between devices  36.3 us (18%)
  matrix products  33.4 us (17%)
  other arithmetic  25 us (12%)
  blocking collectives  11.7 us (6%)
  between operations  2.51 us (1%)
    all_to_all x1, waiting for transfers between devices, fetch_pages(): lax.all_to_all(pool_pages[lax.all_to_all(wanted_slots, 'cache', split_axi...  40.6 us
    ppermute x9, starting transfers between devices, passed_along(): lax.ppermute(value, axis, [(source, source + steps) for source in range(l...  25.9 us
    scatter x1, local copies, waits for them, and re-layouts, fetch_pages(): jnp.zeros((owners_count, capacity), jnp.int32).at[owner_list, ranking]  19.7 us
    dot_general x6, matrix products, attend(): jnp.einsum('qhgd,khd->hgqk', grouped, keys_part, preferred_element_type=j...  17 us
    reduce_sum x6, other arithmetic, attend(): totals = totals * factor + jnp.sum(weights, axis=-1)  11.4 us
    dot_general x6, matrix products, attend(): jnp.einsum('hgqk,khd->hgqd', weights.astype(jnp.bfloat16), values_part, p...  10.5 us
    all_gather x1, blocking collectives, local(): lax.all_gather(page_owner[:, :, :, 0], 'blk', axis=1, tiled=True)  6.28 us
    unnamed x60, local copies, waits for them, and re-layouts  5.84 us
  transfers between devices with their start and end apart: 11, of which 2 were waited for; matrix products, arithmetic and copies ran while one was open for 18% of the time, Pallas kernels for 0%

commit v1 on v0

--- a/solution.py
+++ b/solution.py
@@ -13,6 +13,27 @@
 PAGE = 8
 LIST = 32
 NEG = -1e30
+
+
+def in_order(blocks, dim):
+    lengths = list(blocks.shape[1:])
+    lengths[dim] *= blocks.shape[0]
+    return jnp.moveaxis(blocks, 0, dim).reshape(lengths)
+
+
+def doubled(x, axis):
+    size, mine = (lax.axis_size(axis), lax.axis_index(axis))
+    parts, bit = (x[None], 1)
+    while bit < size:
+        other = lax.ppermute(parts, axis, [(i, i ^ bit) for i in range(size)])
+        low = mine & bit == 0
+        parts = jnp.concatenate([jnp.where(low, parts, other), jnp.where(low, other, parts)])
+        bit *= 2
+    return parts
+
+
+def collect(x, axis, dim):
+    return in_order(doubled(x, axis), dim)
 
 
 def passed_along(value, axis, steps):
@@ -110,7 +131,7 @@
     pool_pages = page_pool[0]
     capacity = max(2, 2 * LIST // lax.axis_size("cache"))
     all_owners, all_slots = (
-        lax.all_gather(page_owner[:, :, :, 0], "blk", axis=1, tiled=True),
+        collect(page_owner[:, :, :, 0], "blk", 1),
         lax.all_gather(page_slot, "blk", axis=1, tiled=True),
     )
     fetched = fetch_pages(

time: 201 us -> 200 us (level)
  blocking collectives: 11.7 us -> 5.7 us
  starting transfers between devices: 36.3 us -> 40.2 us
    all_gather x1 -> x0, blocking collectives: 6.28 us -> none  [local(): lax.all_gather(page_owner[:, :, :, 0], 'blk', axis=1, tiled=True)]
    ppermute x0 -> x2, starting transfers between devices: none -> 3.17 us  [doubled(): other = lax.ppermute(parts, axis, [(i, i ^ bit) for i in range(size)])]
    all_to_all x1, waiting for transfers between devices: 0.01 us -> 3.04 us  [fetch_pages(): lax.all_to_all(wanted_slots, 'cache', split_axis=0, concat_axis=0, tiled=...]
    all_to_all x1, waiting for transfers between devices: 40.6 us -> 37.9 us  [fetch_pages(): lax.all_to_all(pool_pages[lax.all_to_all(wanted_slots, 'cache', split_axi...]
  transfers between devices with their start and end apart: 11 -> 13, of which waited for: 2 -> 4; matrix products, arithmetic and copies ran while one was open for 18% -> 30% of each run, Pallas kernels for 0% -> 0%
where the time goes in v1:
time: 200 us; the launch traced here: 198 us
  local copies, waits for them, and re-layouts  48.5 us (24%)
  waiting for transfers between devices  41.7 us (21%)
  starting transfers between devices  40.2 us (20%)
  matrix products  33.4 us (17%)
  other arithmetic  26.4 us (13%)
  blocking collectives  5.7 us (3%)
  between operations  2.51 us (1%)
    all_to_all x1, waiting for transfers between devices, fetch_pages(): lax.all_to_all(pool_pages[lax.all_to_all(wanted_slots, 'cache', split_axi...  37.9 us
    ppermute x9, starting transfers between devices, passed_along(): lax.ppermute(value, axis, [(source, source + steps) for source in range(l...  27 us
    scatter x1, local copies, waits for them, and re-layouts, fetch_pages(): jnp.zeros((owners_count, capacity), jnp.int32).at[owner_list, ranking]  19.7 us
    dot_general x6, matrix products, attend(): jnp.einsum('qhgd,khd->hgqk', grouped, keys_part, preferred_element_type=j...  16.9 us
    reduce_sum x6, other arithmetic, attend(): totals = totals * factor + jnp.sum(weights, axis=-1)  11.9 us
    dot_general x6, matrix products, attend(): jnp.einsum('hgqk,khd->hgqd', weights.astype(jnp.bfloat16), values_part, p...  10.6 us
    unnamed x60, local copies, waits for them, and re-layouts  5.94 us
    all_gather x1, blocking collectives, local(): lax.all_gather(page_slot, 'blk', axis=1, tiled=True)  5.7 us
  transfers between devices with their start and end apart: 13, of which 4 were waited for; matrix products, arithmetic and copies ran while one was open for 30% of the time, Pallas kernels for 0%

profile of v1, /device:TPU:0, one launch (start us, length us, event | category | flops | bytes accessed | tf_op | source)
XLA Modules:
  0.0 198.4 jit_solution(1327305746925759992)
XLA Ops:
  1.2 1.2 copy.102
  2.4 2.7 %collective-permute-start.2 = (bf16[128,1024]{0,1:T(8,128)(2,1)S(1)}, bf16[128,1024]{0,1:T(8,128)(2,1)}, u32[]{:S(2)}, u32[]{:S(2)}) collective-permute-start(bf16[128,1024]{0,1:T(8,128)(2,1)S(1)} %bitcast.244), channel_id=1, source_target_pairs={{0,1},{1,2},{2,3},{4,5},{5,6},{6,7},{8,9},{9,10},{10,11},{12,13},{... | collective-permute-start | bytes 786440 | tf_op jit(solution)/shard_map/ppermute | solution.py:42
  5.1 5.7 %all_gather.3 = s32[1,4,32]{2,0,1:T(1,128)S(1)} all-gather(s32[1,1,32]{2,0,1:T(1,128)} %bitcast.280), channel_id=1, replica_groups=mesh['groups'=2,'cache'=4,'blk'=4] {'blk'}, dimensions={1}, use_global_device_ids=true | all-gather | bytes 640 | tf_op jit(solution)/shard_map/all_gather | solution.py:135
  12.9 2.7 %collective-permute-start.1 = (s32[2,1,1,32]{3,2,1,0:T(1,128)S(1)}, s32[2,1,1,32]{3,2,1,0:T(1,128)S(1)}, u32[]{:S(2)}, u32[]{:S(2)}) collective-permute-start(s32[2,1,1,32]{3,2,1,0:T(1,128)S(1)} %pad_add_fusion.1), channel_id=1, source_target_pairs={{0,2},{1,3},{2,0},{3,1},{4,6},{5,7},{6,4},{7,5},{8,10},{9,11},{10,... | collective-permute-start | bytes 776 | tf_op jit(solution)/shard_map/ppermute | solution.py:28
  19.0 19.7 %scatter_fusion = s32[4,64]{1,0:T(4,128)} fusion(s32[4,64]{1,0:T(4,128)} %broadcast.351, s32[128]{0:T(128)S(1)} %get-tuple-element.209, s32[128]{0:T(128)S(1)} %reshape.502), kind=kCustom, calls=%fused_computation.2 | custom fusion | bytes 2560 | tf_op jit(solution)/shard_map/scatter | solution.py:84
  38.7 5.0 %all-to-all-start = ((s32[4,1,64]{2,1,0:T(1,128)}), s32[4,1,64]{2,1,0:T(1,128)S(1)}, u32[]{:S(2)}, u32[]{:S(2)}) async-start(s32[4,1,64]{2,1,0:T(1,128)} %bitcast.8), calls=%async_computation | async-start | bytes 4096 | tf_op jit(solution)/shard_map/all_to_all | solution.py:87
  44.3 1.8 collective-permute-start.5
  46.2 3.0 %all-to-all-done = s32[4,1,64]{2,1,0:T(1,128)S(1)} async-done(((s32[4,1,64]{2,1,0:T(1,128)}), s32[4,1,64]{2,1,0:T(1,128)S(1)}, u32[]{:S(2)}, u32[]{:S(2)}) %all-to-all-start) | async-done | bytes 1056 | tf_op jit(solution)/shard_map/all_to_all | solution.py:87
  49.3 2.8 %gather_fusion = bf16[256,8,1024]{2,1,0:T(8,128)(2,1)} fusion(bf16[128,8,1024]{2,1,0:T(8,128)(2,1)S(1)} %bitcast.227, s32[1024]{0:T(1024)S(1)} %pad_clamp_fusion), kind=kCustom, calls=%fused_computation | custom fusion | bytes 8389632 | tf_op jit(solution)/shard_map/gather | solution.py:87
  52.1 5.0 %all-to-all-start.1 = ((bf16[4,64,8,1024]{3,2,1,0:T(8,128)(2,1)}), bf16[4,64,8,1024]{3,2,1,0:T(8,128)(2,1)}, u32[]{:S(2)}, u32[]{:S(2)}) async-start(bf16[4,64,8,1024]{3,2,1,0:T(8,128)(2,1)} %bitcast.235), calls=%async_computation.1 | async-start | bytes 8388608 | tf_op jit(solution)/shard_map/all_to_all | solution.py:86
  59.3 1.3 copy.121
  65.1 2.7 %convolution_bitcast_fusion.1 = f32[128,32,64]{0,2,1:T(8,128)} fusion(bf16[128,32,64]{0,2,1:T(8,128)(2,1)S(1)} %bitcast.238, f32[32,128]{1,0:T(8,128)} %bitcast.276, f32[32,128]{1,0:T(8,128)} %copy.118, f32[128,128]{1,0:T(8,128)S(1)} %fusion.73, pred[128,128]{1,0:T(8,128)(4,1)S(1)} %iota_compare_fusion), kind=kOutput, calls=%fused_computation.46 | convolution fusion | flops 69730304 | bytes 1687552 | tf_op jit(solution)/shard_map/hts,shp->thp/dot_general | solution.py:183
  67.8 2.0 %select_reduce_fusion.3 = (f32[4,4,128]{2,1,0:T(4,128)}, f32[4,4,128,128]{2,3,1,0:T(8,128)}) fusion(pred[128,128]{0,1:T(8,128)(4,1)S(1)} %get-tuple-element.234, bf16[128,4,128,1]{0,2,3,1:T(8,128)(2,1)S(1)} %bitcast.252, bf16[128,4,4,128]{0,3,2,1:T(8,128)(2,1)S(1)} %bitcast.230), kind=kOutput, calls=%fused_computation.70 | convolution fusion | flops 67893248 | bytes 1728512 | tf_op jit(solution)/shard_map/qhgd,khd->hgqk/dot_general | solution.py:59
  71.4 1.3 collective-permute-start.6
  73.5 1.4 add_convert_fusion.2
  74.9 5.2 %collective-permute-start.8 = (bf16[32,64,128]{2,1,0:T(8,128)(2,1)}, bf16[32,64,128]{2,1,0:T(8,128)(2,1)}, u32[]{:S(2)}, u32[]{:S(2)}) collective-permute-start(bf16[32,64,128]{2,1,0:T(8,128)(2,1)} %get-tuple-element.246), channel_id=1, source_target_pairs={{0,1},{1,2},{2,3},{4,5},{5,6},{6,7},{8,9},{9,10},{10,11},{12,13},{... | collective-permute-start | bytes 1572872 | tf_op jit(solution)/shard_map/ppermute | solution.py:42
  80.2 1.0 copy.101
  81.9 3.4 %collective-permute-start.7 = (bf16[32]{0:T(256)(128)(2,1)S(1)}, bf16[32]{0:T(256)(128)(2,1)S(1)}, u32[]{:S(2)}, u32[]{:S(2)}) collective-permute-start(bf16[32]{0:T(256)(128)(2,1)S(1)} %get-tuple-element.227), channel_id=1, source_target_pairs={{0,1},{1,2},{2,3},{4,5},{5,6},{6,7},{8,9},{9,10},{10,11},{12,13},{... | collective-permute-start | bytes 200 | tf_op jit(solution)/shard_map/ppermute | solution.py:42
  85.2 1.5 copy.122
  86.8 3.1 %collective-permute-start.3 = (bf16[128,1024]{0,1:T(8,128)(2,1)}, bf16[128,1024]{0,1:T(8,128)(2,1)S(1)}, u32[]{:S(2)}, u32[]{:S(2)}) collective-permute-start(bf16[128,1024]{0,1:T(8,128)(2,1)} %collective-permute-done.2), channel_id=1, source_target_pairs={{0,1},{1,2},{2,3},{4,5},{5,6},{6,7},{8,9},{9,10},{10,11},{12,13},{... | collective-permute-start | bytes 786440 | tf_op jit(solution)/shard_map/ppermute | solution.py:42
  89.9 1.6 add_convert_fusion.1
  91.5 4.4 %collective-permute-start.9 = (bf16[32,64,128]{2,1,0:T(8,128)(2,1)S(1)}, bf16[32,64,128]{2,1,0:T(8,128)(2,1)S(1)}, u32[]{:S(2)}, u32[]{:S(2)}) collective-permute-start(bf16[32,64,128]{2,1,0:T(8,128)(2,1)S(1)} %add_convert_fusion.1), channel_id=1, source_target_pairs={{0,1},{1,2},{2,3},{4,5},{5,6},{6,7},{8,9},{9,10},{10,11},{12,13},{... | collective-permute-start | bytes 1572872 | tf_op jit(solution)/shard_map/ppermute | solution.py:42
  95.9 1.0 fusion.96
  97.0 1.9 select_reduce_fusion.2
  98.9 1.9 collective-permute-start.4
  101.7 3.2 %collective-permute-start.10 = (bf16[32,64,128]{2,1,0:T(8,128)(2,1)S(1)}, bf16[32,64,128]{2,1,0:T(8,128)(2,1)S(1)}, u32[]{:S(2)}, u32[]{:S(2)}) collective-permute-start(bf16[32,64,128]{2,1,0:T(8,128)(2,1)S(1)} %add_convert_fusion), channel_id=1, source_target_pairs={{0,1},{1,2},{2,3},{4,5},{5,6},{6,7},{8,9},{9,10},{10,11},{12,13},{... | collective-permute-start | bytes 1572872 | tf_op jit(solution)/shard_map/ppermute | solution.py:42
  105.0 2.6 %select_reduce_fusion.1 = (f32[4,4,128]{2,1,0:T(4,128)}, f32[4,4,128,128]{2,3,1,0:T(8,128)}) fusion(pred[128,128]{0,1:T(8,128)(4,1)} %get-tuple-element.235, bf16[128,4,128,1]{0,2,3,1:T(8,128)(2,1)S(1)} %bitcast.251, bf16[128,4,4,128]{0,3,2,1:T(8,128)(2,1)S(1)} %bitcast.233), kind=kOutput, calls=%fused_computation.66 | convolution fusion | flops 67893248 | bytes 1728512 | tf_op jit(solution)/shard_map/qhgd,khd->hgqk/dot_general | solution.py:59
  108.3 2.0 select_reduce_fusion
  111.2 1.0 copy.125
  112.2 37.9 %all-to-all-done.1 = bf16[4,64,8,1024]{3,2,1,0:T(8,128)(2,1)} async-done(((bf16[4,64,8,1024]{3,2,1,0:T(8,128)(2,1)}), bf16[4,64,8,1024]{3,2,1,0:T(8,128)(2,1)}, u32[]{:S(2)}, u32[]{:S(2)}) %all-to-all-start.1) | async-done | bytes 4194336 | tf_op jit(solution)/shard_map/all_to_all | solution.py:86
  150.1 4.4 %gather_fusion.1 = bf16[128,8,1024]{2,1,0:T(8,128)(2,1)} fusion(bf16[4,64,8,1024]{3,2,1,0:T(8,128)(2,1)} %all-to-all-done.1, s32[128]{0:T(128)S(1)} %bitcast.237), kind=kCustom, calls=%fused_computation.1 | custom fusion | bytes 4195328 | tf_op jit(solution)/shard_map/gather | solution.py:93
  154.5 31.0 %while.18 = (s32[]{:T(128)}, f32[4,4,128]{2,1,0:T(4,128)S(1)}, f32[4,4,128]{2,1,0:T(4,128)}, f32[4,4,128,128]{3,2,1,0:T(8,128)}, pred[1024]{0:T(1024)(128)(4,1)S...) while((s32[]{:T(128)}, f32[4,4,128]{2,1,0:T(4,128)S(1)}, ...), condition=%wide.region_6.7_spmd.clone, body=%wide.region_3.6_spmd.clone.sunk | while | flops 549201920 | bytes 20581064 | solution.py:154
  154.6 1.3 fusion.129
  155.8 1.1 copy.163
  156.9 4.2 %fusion.130 = (f32[4,4,128]{2,1,0:T(4,128)S(1)}, f32[4,512,128,4]{2,1,3,0:T(8,128)}) fusion(pred[512]{0:T(512)(128)(4,1)S(1)} %dynamic_slice.17, bf16[512,4,128,1]{0,2,3,1:T(8,128)(2,1)} %bitcast.228, bf16[128,4,4,128]{3,0,2,1:T(8,128)(2,1)} %get-tuple-element.350), kind=kOutput, calls=%fused_computation.5.clone.1 | convolution fusion | flops 271579136 | bytes 5251584 | tf_op jit(solution)/shard_map/while/body/eval_jaxpr/qhgd,khd->hgqk/dot_general | solution.py:59
  161.1 3.1 %fusion.131 = f32[4,4,128]{2,1,0:T(4,128)S(1)} fusion(f32[4,512,128,4]{2,1,3,0:T(8,128)} %get-tuple-element.316, f32[4,4,128]{2,1,0:T(4,128)S(1)} %select_maximum_fusion.2, pred[512]{0:T(512)(128)(4,1)S(1)} %dynamic_slice.17), kind=kLoop, calls=%fused_computation.9.clone.1 | loop fusion | flops 4192256 | bytes 4211200 | tf_op jit(solution)/shard_map/while/body/eval_jaxpr/reduce_sum | solution.py:66
  165.0 4.5 %fusion.133 = f32[4,4,128,128]{3,2,1,0:T(8,128)} fusion(bf16[512,4,128,1]{0,2,3,1:T(8,128)(2,1)S(1)} %bitcast.236, f32[4,512,128,4]{2,1,3,0:T(8,128)} %get-tuple-element.316, f32[4,4,128]{2,1,0:T(4,128)S(1)} %select_maximum_fusion.2, pred[512]{0:T(512)(128)(4,1)S(1)} %dynamic_slice.17, f32[4,4,128,128]{3,2,1,0:T(8,128)} %get-tuple-element.335, ...), kind=kOutput, calls=%fused_computation.15.clone.1 | convolution fusion | flops 273416192 | bytes 6832641 | tf_op jit(solution)/shard_map/while/body/eval_jaxpr/hgqk,khd->hgqd/dot_general | solution.py:67
  169.6 1.3 fusion.129
  170.8 1.1 copy.163
  171.9 4.2 %fusion.130 = (f32[4,4,128]{2,1,0:T(4,128)S(1)}, f32[4,512,128,4]{2,1,3,0:T(8,128)}) fusion(pred[512]{0:T(512)(128)(4,1)S(1)} %dynamic_slice.17, bf16[512,4,128,1]{0,2,3,1:T(8,128)(2,1)} %bitcast.228, bf16[128,4,4,128]{3,0,2,1:T(8,128)(2,1)} %get-tuple-element.350), kind=kOutput, calls=%fused_computation.5.clone.1 | convolution fusion | flops 271579136 | bytes 5251584 | tf_op jit(solution)/shard_map/while/body/eval_jaxpr/qhgd,khd->hgqk/dot_general | solution.py:59
  176.1 3.1 %fusion.131 = f32[4,4,128]{2,1,0:T(4,128)S(1)} fusion(f32[4,512,128,4]{2,1,3,0:T(8,128)} %get-tuple-element.316, f32[4,4,128]{2,1,0:T(4,128)S(1)} %select_maximum_fusion.2, pred[512]{0:T(512)(128)(4,1)S(1)} %dynamic_slice.17), kind=kLoop, calls=%fused_computation.9.clone.1 | loop fusion | flops 4192256 | bytes 4211200 | tf_op jit(solution)/shard_map/while/body/eval_jaxpr/reduce_sum | solution.py:66
  179.1 1.3 fusion.132
  180.7 4.8 %fusion.133 = f32[4,4,128,128]{3,2,1,0:T(8,128)} fusion(bf16[512,4,128,1]{0,2,3,1:T(8,128)(2,1)S(1)} %bitcast.236, f32[4,512,128,4]{2,1,3,0:T(8,128)} %get-tuple-element.316, f32[4,4,128]{2,1,0:T(4,128)S(1)} %select_maximum_fusion.2, pred[512]{0:T(512)(128)(4,1)S(1)} %dynamic_slice.17, f32[4,4,128,128]{3,2,1,0:T(8,128)} %get-tuple-element.335, ...), kind=kOutput, calls=%fused_computation.15.clone.1 | convolution fusion | flops 273416192 | bytes 6832641 | tf_op jit(solution)/shard_map/while/body/eval_jaxpr/hgqk,khd->hgqd/dot_general | solution.py:67
  185.5 2.7 %copy.105 = f32[4,4,128,128]{2,3,1,0:T(8,128)} copy(f32[4,4,128,128]{3,2,1,0:T(8,128)} %get-tuple-element.128) | data formatting | bytes 2097152 | tf_op jit(solution)/shard_map/while | solution.py:154
  189.1 1.4 fusion.41
  190.5 1.4 fusion.43
  192.0 1.4 fusion.45
  193.4 1.5 fusion.47
  (134 shorter events, 23.1 us)
Async XLA Ops:
  0.6 48.7 %copy-start = (bf16[1,128,8,1024]{3,2,1,0:T(8,128)(2,1)S(1)}, bf16[1,128,8,1024]{3,2,1,0:T(8,128)(2,1)}, u32[]{:S(2)}) copy-start(bf16[1,128,8,1024]{3,2,1,0:T(8,128)(2,1)} %param.18) | copy-start | bytes 6291460
  0.6 11.6 %collective-permute-start = (s32[1,1,1,32]{3,2,1,0:T(1,128)}, s32[1,1,1,32]{3,2,1,0:T(1,128)S(1)}, u32[]{:S(2)}, u32[]{:S(2)}) collective-permute-start(s32[1,1,1,32]{3,2,1,0:T(1,128)} %bitcast.281), channel_id=1, source_target_pairs={{0,1},{1,0},{2,3},{3,2},{4,5},{5,4},{6,7},{7,6},{8,9},{9,8},{10,11... | collective-permute-start | bytes 392 | tf_op jit(solution)/shard_map/ppermute | solution.py:28
  2.4 84.4 %collective-permute-start.2 = (bf16[128,1024]{0,1:T(8,128)(2,1)S(1)}, bf16[128,1024]{0,1:T(8,128)(2,1)}, u32[]{:S(2)}, u32[]{:S(2)}) collective-permute-start(bf16[128,1024]{0,1:T(8,128)(2,1)S(1)} %bitcast.244), channel_id=1, source_target_pairs={{0,1},{1,2},{2,3},{4,5},{5,6},{6,7},{8,9},{9,10},{10,11},{12,13},{... | collective-permute-start | bytes 786440 | tf_op jit(solution)/shard_map/ppermute | solution.py:42
  12.9 4.2 %collective-permute-start.1 = (s32[2,1,1,32]{3,2,1,0:T(1,128)S(1)}, s32[2,1,1,32]{3,2,1,0:T(1,128)S(1)}, u32[]{:S(2)}, u32[]{:S(2)}) collective-permute-start(s32[2,1,1,32]{3,2,1,0:T(1,128)S(1)} %pad_add_fusion.1), channel_id=1, source_target_pairs={{0,2},{1,3},{2,0},{3,1},{4,6},{5,7},{6,4},{7,5},{8,10},{9,11},{10,... | collective-permute-start | bytes 776 | tf_op jit(solution)/shard_map/ppermute | solution.py:28
  38.7 10.5 %all-to-all-start = ((s32[4,1,64]{2,1,0:T(1,128)}), s32[4,1,64]{2,1,0:T(1,128)S(1)}, u32[]{:S(2)}, u32[]{:S(2)}) async-start(s32[4,1,64]{2,1,0:T(1,128)} %bitcast.8), calls=%async_computation | async-start | bytes 4096 | tf_op jit(solution)/shard_map/all_to_all | solution.py:87
  44.3 26.4 %collective-permute-start.5 = (bf16[32]{0:T(256)(128)(2,1)}, bf16[32]{0:T(256)(128)(2,1)}, u32[]{:S(2)}, u32[]{:S(2)}) collective-permute-start(bf16[32]{0:T(256)(128)(2,1)} %fusion.89), channel_id=1, source_target_pairs={{0,1},{1,2},{2,3},{4,5},{5,6},{6,7},{8,9},{9,10},{10,11},{12,13},{... | collective-permute-start | bytes 200 | tf_op jit(solution)/shard_map/ppermute | solution.py:42
  52.1 5.5 %copy-start.9 = (bf16[1,128,2048]{2,1,0:T(8,128)(2,1)S(1)}, bf16[1,128,2048]{2,1,0:T(8,128)(2,1)}, u32[]{:S(2)}) copy-start(bf16[1,128,2048]{2,1,0:T(8,128)(2,1)} %param.16) | copy-start | bytes 1572868
  52.1 98.0 %all-to-all-start.1 = ((bf16[4,64,8,1024]{3,2,1,0:T(8,128)(2,1)}), bf16[4,64,8,1024]{3,2,1,0:T(8,128)(2,1)}, u32[]{:S(2)}, u32[]{:S(2)}) async-start(bf16[4,64,8,1024]{3,2,1,0:T(8,128)(2,1)} %bitcast.235), calls=%async_computation.1 | async-start | bytes 8388608 | tf_op jit(solution)/shard_map/all_to_all | solution.py:86
  62.8 7.0 %copy-start.14 = (pred[128,128]{0,1:T(8,128)(4,1)}, pred[128,128]{0,1:T(8,128)(4,1)S(1)}, u32[]{:S(2)}) copy-start(pred[128,128]{0,1:T(8,128)(4,1)S(1)} %get-tuple-element.234) | copy-start | bytes 49156
  64.4 9.0 %copy-start.18 = (bf16[1,128,128]{2,1,0:T(8,128)(2,1)S(1)}, bf16[1,128,128]{2,1,0:T(8,128)(2,1)}, u32[]{:S(2)}) copy-start(bf16[1,128,128]{2,1,0:T(8,128)(2,1)} %param.24) | copy-start | bytes 98308
  67.8 29.2 %copy-start.12 = (pred[128,128]{0,1:T(8,128)(4,1)S(1)}, pred[128,128]{0,1:T(8,128)(4,1)}, u32[]{:S(2)}) copy-start(pred[128,128]{0,1:T(8,128)(4,1)} %get-tuple-element.237) | copy-start | bytes 49156
  71.4 2.1 %collective-permute-start.6 = (bf16[32]{0:T(256)(128)(2,1)S(1)}, bf16[32]{0:T(256)(128)(2,1)S(1)}, u32[]{:S(2)}, u32[]{:S(2)}) collective-permute-start(bf16[32]{0:T(256)(128)(2,1)S(1)} %fusion.78), channel_id=1, source_target_pairs={{0,1},{1,2},{2,3},{4,5},{5,6},{6,7},{8,9},{9,10},{10,11},{12,13},{... | collective-permute-start | bytes 200 | tf_op jit(solution)/shard_map/ppermute | solution.py:42
  73.5 25.4 %copy-start.22 = (f32[32]{0:T(128)}, f32[32]{0:T(128)S(1)}, u32[]{:S(2)}) copy-start(f32[32]{0:T(128)S(1)} %get-tuple-element.229) | copy-start | bytes 388
  74.9 15.0 %collective-permute-start.8 = (bf16[32,64,128]{2,1,0:T(8,128)(2,1)}, bf16[32,64,128]{2,1,0:T(8,128)(2,1)}, u32[]{:S(2)}, u32[]{:S(2)}) collective-permute-start(bf16[32,64,128]{2,1,0:T(8,128)(2,1)} %get-tuple-element.246), channel_id=1, source_target_pairs={{0,1},{1,2},{2,3},{4,5},{5,6},{6,7},{8,9},{9,10},{10,11},{12,13},{... | collective-permute-start | bytes 1572872 | tf_op jit(solution)/shard_map/ppermute | solution.py:42
  80.2 30.1 %copy-start.23 = (pred[128]{0:T(512)(128)(4,1)}, pred[128]{0:T(512)(128)(4,1)S(1)}, u32[]{:S(2)}) copy-start(pred[128]{0:T(512)(128)(4,1)S(1)} %broadcast_compare_fusion.4) | copy-start | bytes 388
  81.9 4.9 %collective-permute-start.7 = (bf16[32]{0:T(256)(128)(2,1)S(1)}, bf16[32]{0:T(256)(128)(2,1)S(1)}, u32[]{:S(2)}, u32[]{:S(2)}) collective-permute-start(bf16[32]{0:T(256)(128)(2,1)S(1)} %get-tuple-element.227), channel_id=1, source_target_pairs={{0,1},{1,2},{2,3},{4,5},{5,6},{6,7},{8,9},{9,10},{10,11},{12,13},{... | collective-permute-start | bytes 200 | tf_op jit(solution)/shard_map/ppermute | solution.py:42
  86.7 14.1 %copy-start.4 = (f32[32,64,128]{2,1,0:T(8,128)S(1)}, f32[32,64,128]{2,1,0:T(8,128)}, u32[]{:S(2)}) copy-start(f32[32,64,128]{2,1,0:T(8,128)} %get-tuple-element.247) | copy-start | bytes 3145732
  86.8 12.2 %collective-permute-start.3 = (bf16[128,1024]{0,1:T(8,128)(2,1)}, bf16[128,1024]{0,1:T(8,128)(2,1)S(1)}, u32[]{:S(2)}, u32[]{:S(2)}) collective-permute-start(bf16[128,1024]{0,1:T(8,128)(2,1)} %collective-permute-done.2), channel_id=1, source_target_pairs={{0,1},{1,2},{2,3},{4,5},{5,6},{6,7},{8,9},{9,10},{10,11},{12,13},{... | collective-permute-start | bytes 786440 | tf_op jit(solution)/shard_map/ppermute | solution.py:42
  89.9 18.4 %copy-start.16 = (pred[128,128]{0,1:T(8,128)(4,1)S(1)}, pred[128,128]{0,1:T(8,128)(4,1)}, u32[]{:S(2)}) copy-start(pred[128,128]{0,1:T(8,128)(4,1)} %get-tuple-element.236) | copy-start | bytes 49156
  91.5 9.4 %collective-permute-start.9 = (bf16[32,64,128]{2,1,0:T(8,128)(2,1)S(1)}, bf16[32,64,128]{2,1,0:T(8,128)(2,1)S(1)}, u32[]{:S(2)}, u32[]{:S(2)}) collective-permute-start(bf16[32,64,128]{2,1,0:T(8,128)(2,1)S(1)} %add_convert_fusion.1), channel_id=1, source_target_pairs={{0,1},{1,2},{2,3},{4,5},{5,6},{6,7},{8,9},{9,10},{10,11},{12,13},{... | collective-permute-start | bytes 1572872 | tf_op jit(solution)/shard_map/ppermute | solution.py:42
  96.9 13.4 %copy-start.7 = (f32[1,32,64,128]{3,2,1,0:T(8,128)S(1)}, f32[1,32,64,128]{3,2,1,0:T(8,128)}, u32[]{:S(2)}) copy-start(f32[1,32,64,128]{3,2,1,0:T(8,128)} %param.29) | copy-start | bytes 3145732
  96.9 13.4 %copy-start.8 = (f32[128,32,64]{0,2,1:T(8,128)S(1)}, f32[128,32,64]{0,2,1:T(8,128)}, u32[]{:S(2)}) copy-start(f32[128,32,64]{0,2,1:T(8,128)} %convolution_bitcast_fusion.1) | copy-start | bytes 3145732
  96.9 13.4 %copy-start.19 = (bf16[1,128,128]{2,1,0:T(8,128)(2,1)S(1)}, bf16[1,128,128]{2,1,0:T(8,128)(2,1)}, u32[]{:S(2)}) copy-start(bf16[1,128,128]{2,1,0:T(8,128)(2,1)} %param.25) | copy-start | bytes 98308
  96.9 13.3 %copy-start.21 = (f32[128,32]{0,1:T(8,128)S(1)}, f32[128,32]{0,1:T(8,128)}, u32[]{:S(2)}) copy-start(f32[128,32]{0,1:T(8,128)} %copy.122) | copy-start | bytes 49156
  97.0 13.3 %copy-start.26 = (f32[32]{0:T(128)S(1)}, f32[32]{0:T(128)}, u32[]{:S(2)}) copy-start(f32[32]{0:T(128)} %param.28) | copy-start | bytes 388
  98.9 8.7 %collective-permute-start.4 = (bf16[128,1024]{0,1:T(8,128)(2,1)S(1)}, bf16[128,1024]{0,1:T(8,128)(2,1)S(1)}, u32[]{:S(2)}, u32[]{:S(2)}) collective-permute-start(bf16[128,1024]{0,1:T(8,128)(2,1)S(1)} %collective-permute-done.3), channel_id=1, source_target_pairs={{0,1},{1,2},{2,3},{4,5},{5,6},{6,7},{8,9},{9,10},{10,11},{12,13},{... | collective-permute-start | bytes 786440 | tf_op jit(solution)/shard_map/ppermute | solution.py:42
  101.7 8.5 %collective-permute-start.10 = (bf16[32,64,128]{2,1,0:T(8,128)(2,1)S(1)}, bf16[32,64,128]{2,1,0:T(8,128)(2,1)S(1)}, u32[]{:S(2)}, u32[]{:S(2)}) collective-permute-start(bf16[32,64,128]{2,1,0:T(8,128)(2,1)S(1)} %add_convert_fusion), channel_id=1, source_target_pairs={{0,1},{1,2},{2,3},{4,5},{5,6},{6,7},{8,9},{9,10},{10,11},{12,13},{... | collective-permute-start | bytes 1572872 | tf_op jit(solution)/shard_map/ppermute | solution.py:42
  110.3 44.2 %copy-start.25 = (pred[1024]{0:T(1024)(128)(4,1)S(1)}, pred[1024]{0:T(1024)(128)(4,1)}, u32[]{:S(2)}) copy-start(pred[1024]{0:T(1024)(128)(4,1)} %lt.128) | copy-start | bytes 3076
  185.5 10.2 %copy-start.1 = (f32[4,4,128,128]{2,3,1,0:T(8,128)S(1)}, f32[4,4,128,128]{2,3,1,0:T(8,128)}, u32[]{:S(2)}) copy-start(f32[4,4,128,128]{2,3,1,0:T(8,128)} %get-tuple-element.245) | copy-start | bytes 3145732
  185.5 10.2 %copy-start.10 = (bf16[128,512]{0,1:T(8,128)(2,1)S(1)}, bf16[128,512]{0,1:T(8,128)(2,1)}, u32[]{:S(2)}) copy-start(bf16[128,512]{0,1:T(8,128)(2,1)} %get-tuple-element.224) | copy-start | bytes 393220
  188.2 7.5 %copy-start.5 = (f32[4,4,128,128]{2,3,1,0:T(8,128)S(1)}, f32[4,4,128,128]{2,3,1,0:T(8,128)}, u32[]{:S(2)}) copy-start(f32[4,4,128,128]{2,3,1,0:T(8,128)} %copy.105) | copy-start | bytes 3145732
  188.2 7.5 %copy-start.15 = (pred[128,128]{0,1:T(8,128)(4,1)S(1)}, pred[128,128]{0,1:T(8,128)(4,1)}, u32[]{:S(2)}) copy-start(pred[128,128]{0,1:T(8,128)(4,1)} %copy-done.14) | copy-start | bytes 49156
  188.2 7.9 %copy-start.2 = (f32[4,4,128,128]{2,3,1,0:T(8,128)S(1)}, f32[4,4,128,128]{2,3,1,0:T(8,128)}, u32[]{:S(2)}) copy-start(f32[4,4,128,128]{2,3,1,0:T(8,128)} %get-tuple-element.243) | copy-start | bytes 3145732
  188.2 7.9 %copy-start.13 = (pred[128,128]{0,1:T(8,128)(4,1)S(1)}, pred[128,128]{0,1:T(8,128)(4,1)}, u32[]{:S(2)}) copy-start(pred[128,128]{0,1:T(8,128)(4,1)} %get-tuple-element.237) | copy-start | bytes 49156
  193.4 3.0 %copy-start.3 = (f32[4,4,128,128]{2,3,1,0:T(8,128)S(1)}, f32[4,4,128,128]{2,3,1,0:T(8,128)}, u32[]{:S(2)}) copy-start(f32[4,4,128,128]{2,3,1,0:T(8,128)} %get-tuple-element.241) | copy-start | bytes 3145732
  193.4 3.0 %copy-start.11 = (pred[128,128]{0,1:T(8,128)(4,1)S(1)}, pred[128,128]{0,1:T(8,128)(4,1)}, u32[]{:S(2)}) copy-start(pred[128,128]{0,1:T(8,128)(4,1)} %get-tuple-element.235) | copy-start | bytes 49156
  195.7 1.2 copy-start.6
  195.7 1.2 copy-start.17
  195.7 1.2 copy-start.20
  196.4 1.1 copy-start.24
